TPU v7x, 256 devices: a whole 4x4x8 slice. The times are simulated.
256 devices in a mesh: expert: 8 (over z_hi, core), cuts: 32 (over y, z_lo, x).
Axes of the slice: x: 4, y: 4, z: 8 (z_hi: 4, z_lo: 2; z = z_hi * 2 + z_lo), core: 2. Of those that a mesh axis runs over, the one named last changes fastest.
Arguments:
- out_grad: bfloat16 [2048, 3072], P(('expert', 'cuts')), may hold values from -6 to 6
- routes: int32 [2048, 2], P(('expert', 'cuts')), may hold values from 0 to 7, all different within a row; in each aligned block of 8 rows (0 to 7, 8 to 15, ...) at most 4 rows name the same one
- gate_weight: float32 [2048, 2], P(('expert', 'cuts')), may hold values from 0.1 to 1
- gate_proj: bfloat16 [8, 3072, 16384], P('expert', None, 'cuts'), may hold values from -0.109375 to 0.109375
- up_proj: bfloat16 [8, 3072, 16384], P('expert', None, 'cuts'), may hold values from -0.109375 to 0.109375
- down_proj: bfloat16 [8, 16384, 3072], P('expert', 'cuts'), may hold values from -0.046875 to 0.046875
- saved_gate: bfloat16 [8, 1024, 16384], P('expert', None, 'cuts'), may hold values from -6 to 6
- saved_up: bfloat16 [8, 1024, 16384], P('expert', None, 'cuts'), may hold values from -6 to 6
Outputs:
- input_grad: bfloat16 [2048, 3072], P(('expert', 'cuts'))
Inputs may be any that keep to these rules, and one draw needn't show every extreme that they name: `routes`: each token names two different experts. Among the 8 tokens of one device no expert is named more than 4 times, and in some devices one expert is named exactly 4 times.
All inputs are finite; a program needn't handle non-finite values.
Results may differ from a plain program's by a relative error of at most 0.0057.
Values may be sent and summed in bfloat16 or wider, within the bound.
No kernel may reach another device: no remote copies, remote signals or barrier semaphores. Data moves between devices by JAX's collectives and lax.ppermute only.
A program may use at most 128 MiB of HBM per device.

v0:
```python
import jax
import jax.numpy as jnp
from jax import lax
from jax.sharding import PartitionSpec as P


def rank_slots(flat_routes):
    count = flat_routes.shape[-1]
    positions = jnp.arange(count, dtype=jnp.int32)
    before = positions[:, None] < positions[None, :]
    matches = flat_routes[..., :, None] == flat_routes[..., None, :]
    return jnp.sum(jnp.logical_and(matches, before), axis=-2)


def expert_rows(grad_rows, gate_mat, up_mat, down_mat, pre_gate, pre_up):
    contract = (((1,), (1,)), ((), ()))
    hidden_grad = lax.dot_general(grad_rows, down_mat, contract, preferred_element_type=jnp.float32)
    gate_vals = pre_gate.astype(jnp.float32)
    up_vals = pre_up.astype(jnp.float32)
    sigmoid_gate = jax.nn.sigmoid(gate_vals)
    up_grad = (hidden_grad * gate_vals * sigmoid_gate).astype(jnp.bfloat16)
    gate_grad = (
        hidden_grad * up_vals * sigmoid_gate * (1.0 + gate_vals * (1.0 - sigmoid_gate))
    ).astype(jnp.bfloat16)
    partial_value = lax.dot_general(
        gate_grad, gate_mat, contract, preferred_element_type=jnp.float32
    )
    return partial_value + lax.dot_general(
        up_grad, up_mat, contract, preferred_element_type=jnp.float32
    )


def shards(out_grad, routes, gate_weight, gate_proj, up_proj, down_proj, saved_gate, saved_up):
    expert_count = lax.axis_size("expert")
    cut_count = lax.axis_size("cuts")
    tok_rows = out_grad.shape[0]
    feature_dim = out_grad.shape[1]
    slot_count = saved_gate.shape[1] // (expert_count * cut_count)
    flat_routes = routes.reshape(-1)
    slot_index = rank_slots(flat_routes[None, :])[0]
    own_spots = flat_routes * slot_count + slot_index
    routed = (gate_weight[:, :, None] * out_grad.astype(jnp.float32)[:, None, :]).astype(
        jnp.bfloat16
    )
    routed = routed.reshape(2 * tok_rows, feature_dim)
    places = jnp.arange(expert_count * slot_count, dtype=jnp.int32)
    placing = (places[:, None] == own_spots[None, :]).astype(jnp.bfloat16)
    outgoing = jnp.dot(placing, routed, preferred_element_type=jnp.float32).astype(jnp.bfloat16)
    outgoing = outgoing.reshape(expert_count, slot_count, feature_dim)
    arrived = lax.all_to_all(outgoing, "expert", split_axis=0, concat_axis=0, tiled=True)
    gathered = lax.all_gather(arrived, "cuts", axis=0, tiled=True).reshape(-1, feature_dim)
    gate_block = saved_gate[0]
    up_block = saved_up[0]
    own_rows = lax.psum_scatter(
        expert_rows(gathered, gate_proj[0], up_proj[0], down_proj[0], gate_block, up_block),
        "cuts",
        scatter_dimension=0,
        tiled=True,
    )
    own_rows = own_rows.reshape(expert_count, slot_count, feature_dim)
    returned = lax.all_to_all(own_rows, "expert", split_axis=0, concat_axis=0, tiled=True).reshape(
        -1, feature_dim
    )
    picked = returned[own_spots].reshape(tok_rows, 2, feature_dim)
    summed = jnp.sum(picked, axis=1)
    return summed.astype(jnp.bfloat16)


def solution(mesh):
    in_specs = (
        P(("expert", "cuts"), None),
        P(("expert", "cuts"), None),
        P(("expert", "cuts"), None),
        P("expert", None, "cuts"),
        P("expert", None, "cuts"),
        P("expert", "cuts", None),
        P("expert", None, "cuts"),
        P("expert", None, "cuts"),
    )
    out_specs = P(("expert", "cuts"), None)
    return jax.shard_map(shards, mesh=mesh, in_specs=in_specs, out_specs=out_specs, check_vma=False)
```

profile of v0, /device:TPU:1, one launch (start us, length us, event | category | flops | bytes accessed | tf_op | source)
XLA Modules:
  0.0 447.9 jit_solution(10655619750516656824)
XLA Ops:
  6.5 0.9 copy.18
  7.4 0.1 reshape.151
  7.5 0.1 convert_reduce_fusion
  7.6 0.9 mul.58
  8.5 0.1 mul.59
  8.6 0.8 copy.19
  9.4 0.1 mul.56
  9.5 0.3 convolution_convert_fusion
  9.8 18.5 %all_to_all.10 = bf16[8,4,3072]{2,1,0:T(4,128)(2,1)} all-to-all(bf16[8,4,3072]{2,1,0:T(4,128)(2,1)S(1)} %reshape.152), channel_id=1, replica_groups=mesh['expert'=8,'cuts'=32] {'expert'}, dimensions={0} | all-to-all | bytes 393216 | tf_op jit(solution)/shard_map/all_to_all | solution.py:50
  28.4 145.1 %all-gather.2.cloned.1.call-done = bf16[256,4,3072]{2,1,0:T(4,128)(2,1)} async-done(((bf16[8,4,3072]{2,1,0:T(4,128)(2,1)}), bf16[256,4,3072]{2,1,0:T(4,128)(2,1)}) %all-gather.2.cloned.1.call-update) | async-done | bytes 6291472 | tf_op jit(solution)/shard_map/all_gather | solution.py:51
  173.5 10.6 %reshape.153 = bf16[1024,3072]{1,0:T(8,128)(2,1)} reshape(bf16[256,4,3072]{2,1,0:T(4,128)(2,1)} %all-gather.2.cloned.1.call-done) | data formatting | bytes 12582912 | tf_op jit(solution)/shard_map/reshape | solution.py:51
  184.2 6.6 %fusion.3 = f32[1024,512]{1,0:T(8,128)S(1)} fusion(bf16[1024,3072]{1,0:T(8,128)(2,1)} %reshape.153, bf16[1,512,3072]{2,1,0:T(8,128)(2,1)} %param.13), kind=kOutput, calls=%fused_computation.9 | convolution fusion | flops 3221225472 | bytes 11534336 | tf_op jit(solution)/shard_map/dot_general | solution.py:17
  190.8 3.9 fusion.1
  194.7 10.5 %convolution_add_fusion = f32[1024,3072]{1,0:T(8,128)} fusion(f32[1024,3072]{1,0:T(8,128)S(1)} %fusion.1, bf16[1,3072,512]{2,1,0:T(8,128)(2,1)} %param.12, f32[1024,512]{1,0:T(8,128)S(1)} %fusion.3, bf16[1,1024,512]{2,1,0:T(8,128)(2,1)} %param.14), kind=kOutput, calls=%fused_computation.1 | convolution fusion | flops 3228041216 | bytes 31457280 | tf_op jit(solution)/shard_map/dot_general | solution.py:28
  205.2 190.7 %reduce-scatter.2.cloned.1.call-done = f32[32,3072]{1,0:T(8,128)} async-done(((f32[1024,3072]{1,0:T(8,128)}), f32[32,3072]{1,0:T(8,128)}) %reduce-scatter.2.cloned.1.call-update) | async-done | bytes 393232 | tf_op jit(solution)/shard_map/reduce_scatter | solution.py:54
  395.9 1.9 reshape.154
  397.8 27.4 %all-to-all-start.1 = ((f32[8,4,3072]{2,1,0:T(4,128)}), f32[8,4,3072]{2,1,0:T(4,128)}, u32[]{:S(2)}, u32[]{:S(2)}) async-start(f32[8,4,3072]{2,1,0:T(4,128)} %reshape.154), calls=%async_computation.2 | async-start | bytes 786432 | tf_op jit(solution)/shard_map/all_to_all | solution.py:61
  425.3 0.1 copy.20
  425.3 0.1 mul.68
  425.4 11.3 %all-to-all-done.1 = f32[8,4,3072]{2,1,0:T(4,128)} async-done(((f32[8,4,3072]{2,1,0:T(4,128)}), f32[8,4,3072]{2,1,0:T(4,128)}, u32[]{:S(2)}, u32[]{:S(2)}) %all-to-all-start.1) | async-done | bytes 393248 | tf_op jit(solution)/shard_map/all_to_all | solution.py:61
  436.7 1.1 reshape.155
  437.9 1.3 gather_fusion
  439.2 1.0 reshape.156
  440.2 0.9 reduce_sum.22
  (17 shorter events, 0.2 us)
Async XLA Ops:
  6.5 184.3 %copy-start = (bf16[1,3072,512]{2,1,0:T(8,128)(2,1)S(1)}, bf16[1,3072,512]{2,1,0:T(8,128)(2,1)}, u32[]{:S(2)}) copy-start(bf16[1,3072,512]{2,1,0:T(8,128)(2,1)} %param.11) | copy-start | bytes 9437188
  6.5 167.0 %all-gather.2.cloned.1.call-start = ((), (), s32[]{:S(2)}) async-start(), calls=%async_computation.3 | async-start | bytes 6488064 | tf_op jit(solution)/shard_map/all_gather | solution.py:51
  28.4 367.6 %reduce-scatter.2.cloned.1.call-start = ((), (), s32[]{:S(2)}) async-start(), calls=%async_computation.4 | async-start | bytes 12976128 | tf_op jit(solution)/shard_map/reduce_scatter | solution.py:54
  184.2 6.7 %copy-start.1 = (bf16[1,1024,512]{2,1,0:T(8,128)(2,1)S(1)}, bf16[1,1024,512]{2,1,0:T(8,128)(2,1)}, u32[]{:S(2)}) copy-start(bf16[1,1024,512]{2,1,0:T(8,128)(2,1)} %param.14) | copy-start | bytes 3145732
  184.2 6.7 %copy-start.3 = (bf16[1,1024,512]{2,1,0:T(8,128)(2,1)S(1)}, bf16[1,1024,512]{2,1,0:T(8,128)(2,1)}, u32[]{:S(2)}) copy-start(bf16[1,1024,512]{2,1,0:T(8,128)(2,1)} %param.15) | copy-start | bytes 3145732
  205.2 220.0 %copy-start.2 = (s32[8,2]{0,1:T(2,128)S(1)}, s32[8,2]{0,1:T(2,128)}, u32[]{:S(2)}) copy-start(s32[8,2]{0,1:T(2,128)} %param.9) | copy-start | bytes 196
  397.8 38.9 %all-to-all-start.1 = ((f32[8,4,3072]{2,1,0:T(4,128)}), f32[8,4,3072]{2,1,0:T(4,128)}, u32[]{:S(2)}, u32[]{:S(2)}) async-start(f32[8,4,3072]{2,1,0:T(4,128)} %reshape.154), calls=%async_computation.2 | async-start | bytes 786432 | tf_op jit(solution)/shard_map/all_to_all | solution.py:61
Sparse Core Ops, SparseCore 0:
  28.5 144.9 all-gather.1
  205.4 190.5 reduce-scatter.1
where the time goes:
time: 448 us
  waiting for transfers between devices  347 us (77%)
  starting transfers between devices  27.5 us (6%)
  matrix products  21.3 us (5%)
  local copies, waits for them, and re-layouts  19 us (4%)
  blocking collectives  18.5 us (4%)
  between operations  13.5 us (3%)
    reduce_scatter x1, waiting for transfers between devices, shards(): lax.psum_scatter(expert_rows(gathered, gate_proj[0], up_proj[0], down_pro...  191 us
    all_gather x1, waiting for transfers between devices, shards(): lax.all_gather(arrived, 'cuts', axis=0, tiled=True).reshape(-1, feature_dim)  145 us
    all_to_all x1, starting transfers between devices, shards(): lax.all_to_all(own_rows, 'expert', split_axis=0, concat_axis=0, tiled=True)  27.4 us
    all_to_all x1, blocking collectives, shards(): lax.all_to_all(outgoing, 'expert', split_axis=0, concat_axis=0, tiled=True)  18.5 us
    all_to_all x1, waiting for transfers between devices, shards(): lax.all_to_all(own_rows, 'expert', split_axis=0, concat_axis=0, tiled=True)  11.3 us
    reshape x1, local copies, waits for them, and re-layouts, shards(): lax.all_gather(arrived, 'cuts', axis=0, tiled=True).reshape(-1, feature_dim)  10.6 us
    dot_general x1, matrix products, expert_rows(): lax.dot_general(up_grad, up_mat, contract, preferred_element_type=jnp.flo...  10.5 us
  transfers between devices with their start and end apart: 3, of which 3 were waited for; matrix products, arithmetic and copies ran while one was open for 0% of the time, Pallas kernels for 0%

commit v1 on v0

v1 whole, which is shorter than its diff:
```python
import jax
import jax.numpy as jnp
from jax import lax
from jax.sharding import Mesh, PartitionSpec as P

BF = jnp.bfloat16
F32 = jnp.float32
Z = ("zh", "core", "zl")


def hop(value, axis, step):
    count = lax.axis_size(axis)
    return lax.ppermute(value, axis, [(i, (i + step) % count) for i in range(count)])


def rank_slots(flat_routes):
    count = flat_routes.shape[-1]
    positions = jnp.arange(count, dtype=jnp.int32)
    before = positions[:, None] < positions[None, :]
    matches = flat_routes[:, None] == flat_routes[None, :]
    return jnp.sum(jnp.logical_and(matches, before), axis=-2)


def expert_rows(grad_rows, gate_mat, up_mat, down_mat, pre_gate, pre_up):
    contract = (((1,), (1,)), ((), ()))
    hidden_grad = lax.dot_general(grad_rows, down_mat, contract, preferred_element_type=F32)
    gate_vals = pre_gate.astype(F32)
    up_vals = pre_up.astype(F32)
    sigmoid_gate = jax.nn.sigmoid(gate_vals)
    up_grad = (hidden_grad * gate_vals * sigmoid_gate).astype(BF)
    gate_grad = (
        hidden_grad * up_vals * sigmoid_gate * (1.0 + gate_vals * (1.0 - sigmoid_gate))
    ).astype(BF)
    partial_value = lax.dot_general(gate_grad, gate_mat, contract, preferred_element_type=F32)
    return partial_value + lax.dot_general(up_grad, up_mat, contract, preferred_element_type=F32)


def rolled(value, axis, start):
    size = value.shape[axis]
    return lax.dynamic_slice_in_dim(jnp.concatenate([value, value], axis), start, size, axis)


def shards(out_grad, routes, gate_weight, gate_proj, up_proj, down_proj, saved_gate, saved_up):
    tok, dim = out_grad.shape
    hidden = saved_gate.shape[2]
    my_x, my_y = lax.axis_index("x"), lax.axis_index("y")
    flat_routes = routes.reshape(-1)
    own_spots = flat_routes * 4 + rank_slots(flat_routes)
    routed = (gate_weight[:, :, None] * out_grad.astype(F32)[:, None, :]).astype(BF)
    routed = routed.reshape(2 * tok, dim)
    places = jnp.arange(64, dtype=jnp.int32)
    spot_of = (places // 8) * 4 + places % 4
    placing = (spot_of[:, None] == own_spots[None, :]).astype(BF)
    outgoing = jnp.dot(placing, routed, preferred_element_type=F32).astype(BF)
    arrived = lax.all_to_all(outgoing.reshape(16, 4, dim), Z, split_axis=0, concat_axis=0, tiled=True)
    arrived = arrived.reshape(2, 4, 2, 4, dim).transpose(0, 2, 1, 3, 4).reshape(2, 32, dim)

    def saved(value, first, second):
        blocks = value[0].reshape(4, 2, 4, 2, 16, hidden)
        blocks = rolled(rolled(blocks, 0, my_y), 2, my_x)
        one = blocks[:, :, :, 0].transpose(0, 2, 1, 3, 4).reshape(4, 128, hidden)
        two = blocks[:, :, :, 1].transpose(2, 0, 1, 3, 4).reshape(4, 128, hidden)
        return one, two

    gates = saved(saved_gate, 0, 1)
    ups = saved(saved_up, 0, 1)

    def spread(value, axis):
        return [value] + [hop(value, axis, -r) for r in (1, 2, 3)]

    first = [jnp.concatenate(spread(arrived[h], a), 0) for h, a in ((0, "x"), (1, "y"))]
    second = [spread(first[h], a) for h, a in ((0, "y"), (1, "x"))]

    parts = {}
    for group in ((0,), (1, 3), (2,)):
        rows = jnp.concatenate([second[h][r] for r in group for h in (0, 1)], 0)
        pre_gate = jnp.concatenate([gates[h][r] for r in group for h in (0, 1)], 0)
        pre_up = jnp.concatenate([ups[h][r] for r in group for h in (0, 1)], 0)
        out = expert_rows(rows, gate_proj[0], up_proj[0], down_proj[0], pre_gate, pre_up)
        for i, (r, h) in enumerate([(r, h) for r in group for h in (0, 1)]):
            parts[h, r] = out[i * 128:(i + 1) * 128]

    def collect(pieces, axis):
        total = pieces[0]
        got = [hop(pieces[r].astype(BF), axis, r) for r in (1, 2, 3)]
        for value in got:
            total = total + value.astype(F32)
        return total

    big = [collect([parts[h, r] for r in range(4)], a) for h, a in ((0, "y"), (1, "x"))]
    small = [
        collect([big[h][r * 32:(r + 1) * 32] for r in range(4)], a) for h, a in ((0, "x"), (1, "y"))
    ]
    back = jnp.stack(small).astype(BF).reshape(2, 2, 4, 4, dim).transpose(0, 2, 1, 3, 4)
    returned = lax.all_to_all(back.reshape(16, 4, dim), Z, split_axis=0, concat_axis=0, tiled=True)
    picking = jnp.sum(
        (spot_of[None, None, :] == own_spots.reshape(tok, 2, 1)).astype(BF), axis=1
    )
    summed = jnp.dot(picking, returned.reshape(64, dim), preferred_element_type=F32)
    return summed.astype(BF)


def solution(mesh):
    fine = Mesh(mesh.devices.reshape(4, 2, 4, 2, 4), ("zh", "core", "y", "zl", "x"))
    expert, cuts = ("zh", "core"), ("y", "zl", "x")
    rows = P(expert + cuts, None)
    in_specs = (
        rows,
        rows,
        rows,
        P(expert, None, cuts),
        P(expert, None, cuts),
        P(expert, cuts, None),
        P(expert, None, cuts),
        P(expert, None, cuts),
    )
    return jax.shard_map(shards, mesh=fine, in_specs=in_specs, out_specs=rows, check_vma=False)
```

time: 448 us -> 184 us (0.41)
  the two profiles are of different devices: /device:TPU:1 before, /device:TPU:24 now
where the time goes in v1:
time: 184 us; the launch traced here: 182 us
  waiting for transfers between devices  86.1 us (47%)
  starting transfers between devices  48.9 us (27%)
  local copies, waits for them, and re-layouts  18.7 us (10%)
  matrix products  15.1 us (8%)
  other arithmetic  12.4 us (7%)
    ppermute x24, waiting for transfers between devices, hop(): lax.ppermute(value, axis, [(i, (i + step) % count) for i in range(count)])  71.9 us
    ppermute x24, starting transfers between devices, hop(): lax.ppermute(value, axis, [(i, (i + step) % count) for i in range(count)])  32.7 us
    all_to_all x1, waiting for transfers between devices, shards(): lax.all_to_all(back.reshape(16, 4, dim), Z, split_axis=0, concat_axis=0,...  12.5 us
    all_to_all x1, starting transfers between devices, shards(): lax.all_to_all(outgoing.reshape(16, 4, dim), Z, split_axis=0, concat_axis...  8.57 us
    all_to_all x1, starting transfers between devices, shards(): lax.all_to_all(back.reshape(16, 4, dim), Z, split_axis=0, concat_axis=0,...  7.69 us
    concatenate x3, other arithmetic, rolled(): jnp.concatenate([value, value], axis)  7.49 us
    unnamed x43, local copies, waits for them, and re-layouts  7.41 us
    dot_general x3, matrix products, expert_rows(): lax.dot_general(gate_grad, gate_mat, contract, preferred_element_type=F32)  4.24 us
  transfers between devices with their start and end apart: 26, of which 15 were waited for; matrix products, arithmetic and copies ran while one was open for 16% of the time, Pallas kernels for 0%

profile of v1, /device:TPU:24, one launch (start us, length us, event | category | flops | bytes accessed | tf_op | source)
XLA Modules:
  0.0 181.8 jit_solution(2989278937428172188)
XLA Ops:
  5.8 8.6 %all-to-all-start = ((bf16[16,4,3072]{2,1,0:T(4,128)(2,1)}), bf16[16,4,3072]{2,1,0:T(4,128)(2,1)S(1)}, u32[]{:S(2)}, u32[]{:S(2)}) async-start(bf16[16,4,3072]{2,1,0:T(4,128)(2,1)} %reshape.128), calls=%async_computation | async-start | bytes 786432 | tf_op jit(solution)/shard_map/all_to_all | solution.py:55
  14.3 2.6 %fusion.39 = bf16[4,2,4,2,16,512]{5,4,3,2,1,0:T(8,128)(2,1)} fusion(s32[]{:T(128)S(6)} %select_n.42, bf16[4,2,4,2,16,512]{5,4,3,2,1,0:T(8,128)(2,1)} %bitcast.74), kind=kLoop, calls=%fused_computation.57 | loop fusion | flops 524288 | bytes 2097156 | tf_op jit(solution)/shard_map/concatenate | solution.py:40
  17.0 2.6 %fusion.41 = bf16[4,2,4,2,16,512]{5,4,3,2,1,0:T(8,128)(2,1)} fusion(s32[]{:T(128)S(6)} %select_n.42, bf16[4,2,4,2,16,512]{5,4,3,2,1,0:T(8,128)(2,1)} %bitcast.75), kind=kLoop, calls=%fused_computation.59 | loop fusion | flops 524288 | bytes 2097156 | tf_op jit(solution)/shard_map/concatenate | solution.py:40
  19.5 2.3 %fusion.38 = (bf16[4,2,4,2,16,512]{5,4,3,2,1,0:T(8,128)(2,1)S(1)}, bf16[4,2,4,2,16,512]{5,4,3,2,1,0:T(8,128)(2,1)S(1)}) fusion(s32[]{:T(128)S(6)} %select_n.43, bf16[4,2,4,2,16,512]{5,4,3,2,1,0:T(8,128)(2,1)} %fusion.39, bf16[4,2,4,2,16,512]{5,4,3,2,1,0:T(8,128)(2,1)} %fusion.41), kind=kLoop, calls=%fused_computation.56 | loop fusion | flops 1048576 | bytes 4194308 | tf_op jit(solution)/shard_map/concatenate | solution.py:40
  28.7 2.8 %collective-permute-start = (bf16[32,3072]{1,0:T(8,128)(2,1)}, bf16[32,3072]{1,0:T(8,128)(2,1)}, u32[]{:S(2)}, u32[]{:S(2)}) collective-permute-start(bf16[32,3072]{1,0:T(8,128)(2,1)} %squeeze.81), channel_id=1, source_target_pairs={{0,3},{1,0},{2,1},{3,2},{4,7},{5,4},{6,5},{7,6},{8,11},{9,8},{10,9... | collective-permute-start | bytes 589832 | tf_op jit(solution)/shard_map/ppermute | solution.py:13
  36.9 4.0 %collective-permute-done = bf16[32,3072]{1,0:T(8,128)(2,1)} collective-permute-done((bf16[32,3072]{1,0:T(8,128)(2,1)}, bf16[32,3072]{1,0:T(8,128)(2,1)}, u32[]{:S(2)}, u32[]{:S(2)}) %collective-permute-start) | collective-permute-done | bytes 196640 | tf_op jit(solution)/shard_map/ppermute | solution.py:13
  48.8 2.7 %collective-permute-start.7 = (bf16[128,3072]{1,0:T(8,128)(2,1)S(1)}, bf16[128,3072]{1,0:T(8,128)(2,1)S(1)}, u32[]{:S(2)}, u32[]{:S(2)}) collective-permute-start(bf16[128,3072]{1,0:T(8,128)(2,1)S(1)} %get-tuple-element.46), channel_id=1, source_target_pairs={{0,3},{1,0},{2,1},{3,2},{4,7},{5,4},{6,5},{7,6},{8,11},{9,8},{10,9... | collective-permute-start | bytes 2359304 | tf_op jit(solution)/shard_map/ppermute | solution.py:13
  56.3 12.6 %collective-permute-done.9 = bf16[128,3072]{1,0:T(8,128)(2,1)S(1)} collective-permute-done((bf16[128,3072]{1,0:T(8,128)(2,1)S(1)}, bf16[128,3072]{1,0:T(8,128)(2,1)S(1)}, u32[]{:S(2)}, u32[]{:S(2)}) %collective-permute-start.9) | collective-permute-done | bytes 786464 | tf_op jit(solution)/shard_map/ppermute | solution.py:13
  70.1 14.1 %collective-permute-done.7 = bf16[128,3072]{1,0:T(8,128)(2,1)S(1)} collective-permute-done((bf16[128,3072]{1,0:T(8,128)(2,1)S(1)}, bf16[128,3072]{1,0:T(8,128)(2,1)S(1)}, u32[]{:S(2)}, u32[]{:S(2)}) %collective-permute-start.7) | collective-permute-done | bytes 786464 | tf_op jit(solution)/shard_map/ppermute | solution.py:13
  84.2 5.6 %collective-permute-done.6 = bf16[128,3072]{1,0:T(8,128)(2,1)S(1)} collective-permute-done((bf16[128,3072]{1,0:T(8,128)(2,1)S(1)}, bf16[128,3072]{1,0:T(8,128)(2,1)S(1)}, u32[]{:S(2)}, u32[]{:S(2)}) %collective-permute-start.6) | collective-permute-done | bytes 786464 | tf_op jit(solution)/shard_map/ppermute | solution.py:13
  91.7 2.0 %fusion.14 = f32[512,3072]{1,0:T(8,128)S(1)} fusion(bf16[1,3072,512]{2,1,0:T(8,128)(2,1)S(1)} %copy-done, f32[512,512]{1,0:T(8,128)S(1)} %fusion.1, bf16[128,512]{1,0:T(8,128)(2,1)S(1)} %bitcast.88, bf16[128,512]{1,0:T(8,128)(2,1)S(1)} %bitcast.90, bf16[128,512]{1,0:T(8,128)(2,1)S(1)} %bitcast.89, bf16[128,512]{1,0:T(8,128)(2,1)S(1)} %bitcast.91, ...), kind=kOutput, calls=%fused_computation.19 | convolution fusion | flops 1617428480 | bytes 11534336 | tf_op jit(solution)/shard_map/dot_general | solution.py:34
  93.7 1.9 %add_convert_fusion = bf16[512,3072]{1,0:T(8,128)(2,1)S(1)} fusion(f32[512,3072]{1,0:T(8,128)S(1)} %fusion.14, bf16[1,3072,512]{2,1,0:T(8,128)(2,1)S(1)} %copy-done.1, f32[512,512]{1,0:T(8,128)S(1)} %fusion.1, bf16[128,512]{1,0:T(8,128)(2,1)S(1)} %bitcast.93, bf16[128,512]{1,0:T(8,128)(2,1)S(1)} %bitcast.97, bf16[128,512]{1,0:T(8,128)(2,1)S(1)} %bitcast.95, ...), kind=kOutput, calls=%fused_computation | convolution fusion | flops 1617428480 | bytes 14155776 | tf_op jit(solution)/shard_map/dot_general | solution.py:35
  100.0 2.8 %collective-permute-start.10 = (bf16[128,3072]{1,0:T(8,128)(2,1)S(1)}, bf16[128,3072]{1,0:T(8,128)(2,1)S(1)}, u32[]{:S(2)}, u32[]{:S(2)}) collective-permute-start(bf16[128,3072]{1,0:T(8,128)(2,1)S(1)} %get-tuple-element.11), channel_id=1, source_target_pairs={{0,8},{8,16},{16,24},{24,0},{1,9},{9,17},{17,25},{25,1},{2,10},{10... | collective-permute-start | bytes 2359304 | tf_op jit(solution)/shard_map/ppermute | solution.py:13
  102.9 3.6 %collective-permute-start.19 = (bf16[128,3072]{1,0:T(8,128)(2,1)S(1)}, bf16[128,3072]{1,0:T(8,128)(2,1)S(1)}, u32[]{:S(2)}, u32[]{:S(2)}) collective-permute-start(bf16[128,3072]{1,0:T(8,128)(2,1)S(1)} %get-tuple-element.16), channel_id=1, source_target_pairs={{0,2},{1,3},{2,0},{3,1},{4,6},{5,7},{6,4},{7,5},{8,10},{9,11},{10,... | collective-permute-start | bytes 2359304 | tf_op jit(solution)/shard_map/ppermute | solution.py:13
  106.5 16.2 %collective-permute-done.14 = bf16[128,3072]{1,0:T(8,128)(2,1)S(1)} collective-permute-done((bf16[128,3072]{1,0:T(8,128)(2,1)S(1)}, bf16[128,3072]{1,0:T(8,128)(2,1)S(1)}, u32[]{:S(2)}, u32[]{:S(2)}) %collective-permute-start.14) | collective-permute-done | bytes 786464 | tf_op jit(solution)/shard_map/ppermute | solution.py:13
  126.1 9.8 %collective-permute-done.18 = bf16[128,3072]{1,0:T(8,128)(2,1)S(1)} collective-permute-done((bf16[128,3072]{1,0:T(8,128)(2,1)S(1)}, bf16[128,3072]{1,0:T(8,128)(2,1)S(1)}, u32[]{:S(2)}, u32[]{:S(2)}) %collective-permute-start.18) | collective-permute-done | bytes 786464 | tf_op jit(solution)/shard_map/ppermute | solution.py:13
  135.9 2.1 %fusion.111 = (bf16[128,3072]{1,0:T(8,128)(2,1)S(1)}, f32[128,3072]{1,0:T(8,128)}, bf16[128,3072]{1,0:T(8,128)(2,1)S(1)}, f32[128,3072]{1,0:T(8,128)S(1)}) fusion(bf16[128,3072]{1,0:T(8,128)(2,1)S(1)} %collective-permute-done.14, bf16[128,3072]{1,0:T(8,128)(2,1)S(1)} %collective-permute-done.13, bf16[128,3072]{1,0:T(8,128)(2,1)S(1)} %collective-permute-done.10, ...), kind=kLoop, calls=%fused_computation.167 | loop fusion | flops 5505024 | bytes 12582912 | tf_op jit(solution)/shard_map/convert.13
  139.2 2.2 %collective-permute-start.21 = (bf16[32,3072]{1,0:T(8,128)(2,1)S(1)}, bf16[32,3072]{1,0:T(8,128)(2,1)S(1)}, u32[]{:S(2)}, u32[]{:S(2)}) collective-permute-start(bf16[32,3072]{1,0:T(8,128)(2,1)S(1)} %get-tuple-element.24), channel_id=1, source_target_pairs={{0,8},{8,16},{16,24},{24,0},{1,9},{9,17},{17,25},{25,1},{2,10},{10... | collective-permute-start | bytes 589832 | tf_op jit(solution)/shard_map/ppermute | solution.py:13
  142.6 3.4 %collective-permute-start.16 = (bf16[32,3072]{1,0:T(8,128)(2,1)}, bf16[32,3072]{1,0:T(8,128)(2,1)}, u32[]{:S(2)}, u32[]{:S(2)}) collective-permute-start(bf16[32,3072]{1,0:T(8,128)(2,1)} %get-tuple-element.23), channel_id=1, source_target_pairs={{0,2},{1,3},{2,0},{3,1},{4,6},{5,7},{6,4},{7,5},{8,10},{9,11},{10,... | collective-permute-start | bytes 589832 | tf_op jit(solution)/shard_map/ppermute | solution.py:13
  147.2 2.0 %collective-permute-start.15 = (bf16[32,3072]{1,0:T(8,128)(2,1)}, bf16[32,3072]{1,0:T(8,128)(2,1)}, u32[]{:S(2)}, u32[]{:S(2)}) collective-permute-start(bf16[32,3072]{1,0:T(8,128)(2,1)} %get-tuple-element.21), channel_id=1, source_target_pairs={{0,1},{1,2},{2,3},{3,0},{4,5},{5,6},{6,7},{7,4},{8,9},{9,10},{10,1... | collective-permute-start | bytes 589832 | tf_op jit(solution)/shard_map/ppermute | solution.py:13
  149.9 2.3 %collective-permute-done.16 = bf16[32,3072]{1,0:T(8,128)(2,1)} collective-permute-done((bf16[32,3072]{1,0:T(8,128)(2,1)}, bf16[32,3072]{1,0:T(8,128)(2,1)}, u32[]{:S(2)}, u32[]{:S(2)}) %collective-permute-start.16) | collective-permute-done | bytes 196640 | tf_op jit(solution)/shard_map/ppermute | solution.py:13
  152.2 2.4 %collective-permute-done.15 = bf16[32,3072]{1,0:T(8,128)(2,1)} collective-permute-done((bf16[32,3072]{1,0:T(8,128)(2,1)}, bf16[32,3072]{1,0:T(8,128)(2,1)}, u32[]{:S(2)}, u32[]{:S(2)}) %collective-permute-start.15) | collective-permute-done | bytes 196640 | tf_op jit(solution)/shard_map/ppermute | solution.py:13
  158.8 7.7 %all-to-all-start.1 = ((bf16[16,4,3072]{2,1,0:T(4,128)(2,1)}), bf16[16,4,3072]{2,1,0:T(4,128)(2,1)S(1)}, u32[]{:S(2)}, u32[]{:S(2)}) async-start(bf16[16,4,3072]{2,1,0:T(4,128)(2,1)} %bitcast.73), calls=%async_computation.1 | async-start | bytes 786432 | tf_op jit(solution)/shard_map/all_to_all | solution.py:95
  166.7 12.5 %all-to-all-done.1 = bf16[16,4,3072]{2,1,0:T(4,128)(2,1)S(1)} async-done(((bf16[16,4,3072]{2,1,0:T(4,128)(2,1)}), bf16[16,4,3072]{2,1,0:T(4,128)(2,1)S(1)}, u32[]{:S(2)}, u32[]{:S(2)}) %all-to-all-start.1) | async-done | bytes 393248 | tf_op jit(solution)/shard_map/all_to_all | solution.py:95
  (121 shorter events, 52.7 us)
Async XLA Ops:
  5.8 21.3 %all-to-all-start = ((bf16[16,4,3072]{2,1,0:T(4,128)(2,1)}), bf16[16,4,3072]{2,1,0:T(4,128)(2,1)S(1)}, u32[]{:S(2)}, u32[]{:S(2)}) async-start(bf16[16,4,3072]{2,1,0:T(4,128)(2,1)} %reshape.128), calls=%async_computation | async-start | bytes 786432 | tf_op jit(solution)/shard_map/all_to_all | solution.py:55
  28.7 12.2 %collective-permute-start = (bf16[32,3072]{1,0:T(8,128)(2,1)}, bf16[32,3072]{1,0:T(8,128)(2,1)}, u32[]{:S(2)}, u32[]{:S(2)}) collective-permute-start(bf16[32,3072]{1,0:T(8,128)(2,1)} %squeeze.81), channel_id=1, source_target_pairs={{0,3},{1,0},{2,1},{3,2},{4,7},{5,4},{6,5},{7,6},{8,11},{9,8},{10,9... | collective-permute-start | bytes 589832 | tf_op jit(solution)/shard_map/ppermute | solution.py:13
  31.5 10.7 %collective-permute-start.1 = (bf16[32,3072]{1,0:T(8,128)(2,1)}, bf16[32,3072]{1,0:T(8,128)(2,1)}, u32[]{:S(2)}, u32[]{:S(2)}) collective-permute-start(bf16[32,3072]{1,0:T(8,128)(2,1)} %squeeze.81), channel_id=1, source_target_pairs={{0,2},{1,3},{2,0},{3,1},{4,6},{5,7},{6,4},{7,5},{8,10},{9,11},{10,... | collective-permute-start | bytes 589832 | tf_op jit(solution)/shard_map/ppermute | solution.py:13
  32.3 12.4 %collective-permute-start.2 = (bf16[32,3072]{1,0:T(8,128)(2,1)}, bf16[32,3072]{1,0:T(8,128)(2,1)}, u32[]{:S(2)}, u32[]{:S(2)}) collective-permute-start(bf16[32,3072]{1,0:T(8,128)(2,1)} %squeeze.81), channel_id=1, source_target_pairs={{0,1},{1,2},{2,3},{3,0},{4,5},{5,6},{6,7},{7,4},{8,9},{9,10},{10,1... | collective-permute-start | bytes 589832 | tf_op jit(solution)/shard_map/ppermute | solution.py:13
  34.2 12.1 %collective-permute-start.3 = (bf16[32,3072]{1,0:T(8,128)(2,1)S(1)}, bf16[32,3072]{1,0:T(8,128)(2,1)S(1)}, u32[]{:S(2)}, u32[]{:S(2)}) collective-permute-start(bf16[32,3072]{1,0:T(8,128)(2,1)S(1)} %squeeze.82), channel_id=1, source_target_pairs={{0,24},{8,0},{16,8},{24,16},{1,25},{9,1},{17,9},{25,17},{2,26},{10... | collective-permute-start | bytes 589832 | tf_op jit(solution)/shard_map/ppermute | solution.py:13
  35.0 11.3 %collective-permute-start.4 = (bf16[32,3072]{1,0:T(8,128)(2,1)S(1)}, bf16[32,3072]{1,0:T(8,128)(2,1)S(1)}, u32[]{:S(2)}, u32[]{:S(2)}) collective-permute-start(bf16[32,3072]{1,0:T(8,128)(2,1)S(1)} %squeeze.82), channel_id=1, source_target_pairs={{0,16},{8,24},{16,0},{24,8},{1,17},{9,25},{17,1},{25,9},{2,18},{10... | collective-permute-start | bytes 589832 | tf_op jit(solution)/shard_map/ppermute | solution.py:13
  47.4 21.5 %collective-permute-start.9 = (bf16[128,3072]{1,0:T(8,128)(2,1)S(1)}, bf16[128,3072]{1,0:T(8,128)(2,1)S(1)}, u32[]{:S(2)}, u32[]{:S(2)}) collective-permute-start(bf16[128,3072]{1,0:T(8,128)(2,1)S(1)} %get-tuple-element.46), channel_id=1, source_target_pairs={{0,1},{1,2},{2,3},{3,0},{4,5},{5,6},{6,7},{7,4},{8,9},{9,10},{10,1... | collective-permute-start | bytes 2359304 | tf_op jit(solution)/shard_map/ppermute | solution.py:13
  48.8 35.4 %collective-permute-start.7 = (bf16[128,3072]{1,0:T(8,128)(2,1)S(1)}, bf16[128,3072]{1,0:T(8,128)(2,1)S(1)}, u32[]{:S(2)}, u32[]{:S(2)}) collective-permute-start(bf16[128,3072]{1,0:T(8,128)(2,1)S(1)} %get-tuple-element.46), channel_id=1, source_target_pairs={{0,3},{1,0},{2,1},{3,2},{4,7},{5,4},{6,5},{7,6},{8,11},{9,8},{10,9... | collective-permute-start | bytes 2359304 | tf_op jit(solution)/shard_map/ppermute | solution.py:13
  51.4 18.7 %collective-permute-start.8 = (bf16[128,3072]{1,0:T(8,128)(2,1)S(1)}, bf16[128,3072]{1,0:T(8,128)(2,1)S(1)}, u32[]{:S(2)}, u32[]{:S(2)}) collective-permute-start(bf16[128,3072]{1,0:T(8,128)(2,1)S(1)} %get-tuple-element.54), channel_id=1, source_target_pairs={{0,8},{8,16},{16,24},{24,0},{1,9},{9,17},{17,25},{25,1},{2,10},{10... | collective-permute-start | bytes 2359304 | tf_op jit(solution)/shard_map/ppermute | solution.py:13
  52.9 36.9 %collective-permute-start.6 = (bf16[128,3072]{1,0:T(8,128)(2,1)S(1)}, bf16[128,3072]{1,0:T(8,128)(2,1)S(1)}, u32[]{:S(2)}, u32[]{:S(2)}) collective-permute-start(bf16[128,3072]{1,0:T(8,128)(2,1)S(1)} %get-tuple-element.54), channel_id=1, source_target_pairs={{0,24},{8,0},{16,8},{24,16},{1,25},{9,1},{17,9},{25,17},{2,26},{10... | collective-permute-start | bytes 2359304 | tf_op jit(solution)/shard_map/ppermute | solution.py:13
  53.6 42.4 %collective-permute-start.12 = (bf16[128,3072]{1,0:T(8,128)(2,1)S(1)}, bf16[128,3072]{1,0:T(8,128)(2,1)S(1)}, u32[]{:S(2)}, u32[]{:S(2)}) collective-permute-start(bf16[128,3072]{1,0:T(8,128)(2,1)S(1)} %get-tuple-element.46), channel_id=1, source_target_pairs={{0,2},{1,3},{2,0},{3,1},{4,6},{5,7},{6,4},{7,5},{8,10},{9,11},{10,... | collective-permute-start | bytes 2359304 | tf_op jit(solution)/shard_map/ppermute | solution.py:13
  68.9 27.1 %collective-permute-start.11 = (bf16[128,3072]{1,0:T(8,128)(2,1)S(1)}, bf16[128,3072]{1,0:T(8,128)(2,1)S(1)}, u32[]{:S(2)}, u32[]{:S(2)}) collective-permute-start(bf16[128,3072]{1,0:T(8,128)(2,1)S(1)} %get-tuple-element.54), channel_id=1, source_target_pairs={{0,16},{8,24},{16,0},{24,8},{1,17},{9,25},{17,1},{25,9},{2,18},{10... | collective-permute-start | bytes 2359304 | tf_op jit(solution)/shard_map/ppermute | solution.py:13
  95.9 26.8 %collective-permute-start.14 = (bf16[128,3072]{1,0:T(8,128)(2,1)S(1)}, bf16[128,3072]{1,0:T(8,128)(2,1)S(1)}, u32[]{:S(2)}, u32[]{:S(2)}) collective-permute-start(bf16[128,3072]{1,0:T(8,128)(2,1)S(1)} %get-tuple-element.14), channel_id=1, source_target_pairs={{0,24},{8,0},{16,8},{24,16},{1,25},{9,1},{17,9},{25,17},{2,26},{10... | collective-permute-start | bytes 2359304 | tf_op jit(solution)/shard_map/ppermute | solution.py:13
  99.4 26.7 %collective-permute-start.13 = (bf16[128,3072]{1,0:T(8,128)(2,1)S(1)}, bf16[128,3072]{1,0:T(8,128)(2,1)S(1)}, u32[]{:S(2)}, u32[]{:S(2)}) collective-permute-start(bf16[128,3072]{1,0:T(8,128)(2,1)S(1)} %get-tuple-element.15), channel_id=1, source_target_pairs={{0,16},{8,24},{16,0},{24,8},{1,17},{9,25},{17,1},{25,9},{2,18},{10... | collective-permute-start | bytes 2359304 | tf_op jit(solution)/shard_map/ppermute | solution.py:13
  100.0 26.1 %collective-permute-start.10 = (bf16[128,3072]{1,0:T(8,128)(2,1)S(1)}, bf16[128,3072]{1,0:T(8,128)(2,1)S(1)}, u32[]{:S(2)}, u32[]{:S(2)}) collective-permute-start(bf16[128,3072]{1,0:T(8,128)(2,1)S(1)} %get-tuple-element.11), channel_id=1, source_target_pairs={{0,8},{8,16},{16,24},{24,0},{1,9},{9,17},{17,25},{25,1},{2,10},{10... | collective-permute-start | bytes 2359304 | tf_op jit(solution)/shard_map/ppermute | solution.py:13
  102.8 23.3 %collective-permute-start.20 = (bf16[128,3072]{1,0:T(8,128)(2,1)S(1)}, bf16[128,3072]{1,0:T(8,128)(2,1)S(1)}, u32[]{:S(2)}, u32[]{:S(2)}) collective-permute-start(bf16[128,3072]{1,0:T(8,128)(2,1)S(1)} %get-tuple-element.12), channel_id=1, source_target_pairs={{0,3},{1,0},{2,1},{3,2},{4,7},{5,4},{6,5},{7,6},{8,11},{9,8},{10,9... | collective-permute-start | bytes 2359304 | tf_op jit(solution)/shard_map/ppermute | solution.py:13
  102.9 23.2 %collective-permute-start.19 = (bf16[128,3072]{1,0:T(8,128)(2,1)S(1)}, bf16[128,3072]{1,0:T(8,128)(2,1)S(1)}, u32[]{:S(2)}, u32[]{:S(2)}) collective-permute-start(bf16[128,3072]{1,0:T(8,128)(2,1)S(1)} %get-tuple-element.16), channel_id=1, source_target_pairs={{0,2},{1,3},{2,0},{3,1},{4,6},{5,7},{6,4},{7,5},{8,10},{9,11},{10,... | collective-permute-start | bytes 2359304 | tf_op jit(solution)/shard_map/ppermute | solution.py:13
  122.7 13.2 %collective-permute-start.18 = (bf16[128,3072]{1,0:T(8,128)(2,1)S(1)}, bf16[128,3072]{1,0:T(8,128)(2,1)S(1)}, u32[]{:S(2)}, u32[]{:S(2)}) collective-permute-start(bf16[128,3072]{1,0:T(8,128)(2,1)S(1)} %get-tuple-element.13), channel_id=1, source_target_pairs={{0,1},{1,2},{2,3},{3,0},{4,5},{5,6},{6,7},{7,4},{8,9},{9,10},{10,1... | collective-permute-start | bytes 2359304 | tf_op jit(solution)/shard_map/ppermute | solution.py:13
  138.1 9.1 %collective-permute-start.23 = (bf16[32,3072]{1,0:T(8,128)(2,1)S(1)}, bf16[32,3072]{1,0:T(8,128)(2,1)S(1)}, u32[]{:S(2)}, u32[]{:S(2)}) collective-permute-start(bf16[32,3072]{1,0:T(8,128)(2,1)S(1)} %get-tuple-element.25), channel_id=1, source_target_pairs={{0,24},{8,0},{16,8},{24,16},{1,25},{9,1},{17,9},{25,17},{2,26},{10... | collective-permute-start | bytes 589832 | tf_op jit(solution)/shard_map/ppermute | solution.py:13
  138.2 10.9 %collective-permute-start.22 = (bf16[32,3072]{1,0:T(8,128)(2,1)S(1)}, bf16[32,3072]{1,0:T(8,128)(2,1)S(1)}, u32[]{:S(2)}, u32[]{:S(2)}) collective-permute-start(bf16[32,3072]{1,0:T(8,128)(2,1)S(1)} %get-tuple-element.26), channel_id=1, source_target_pairs={{0,16},{8,24},{16,0},{24,8},{1,17},{9,25},{17,1},{25,9},{2,18},{10... | collective-permute-start | bytes 589832 | tf_op jit(solution)/shard_map/ppermute | solution.py:13
  139.2 10.0 %collective-permute-start.21 = (bf16[32,3072]{1,0:T(8,128)(2,1)S(1)}, bf16[32,3072]{1,0:T(8,128)(2,1)S(1)}, u32[]{:S(2)}, u32[]{:S(2)}) collective-permute-start(bf16[32,3072]{1,0:T(8,128)(2,1)S(1)} %get-tuple-element.24), channel_id=1, source_target_pairs={{0,8},{8,16},{16,24},{24,0},{1,9},{9,17},{17,25},{25,1},{2,10},{10... | collective-permute-start | bytes 589832 | tf_op jit(solution)/shard_map/ppermute | solution.py:13
  142.3 7.7 %collective-permute-start.17 = (bf16[32,3072]{1,0:T(8,128)(2,1)}, bf16[32,3072]{1,0:T(8,128)(2,1)}, u32[]{:S(2)}, u32[]{:S(2)}) collective-permute-start(bf16[32,3072]{1,0:T(8,128)(2,1)} %get-tuple-element.22), channel_id=1, source_target_pairs={{0,3},{1,0},{2,1},{3,2},{4,7},{5,4},{6,5},{7,6},{8,11},{9,8},{10,9... | collective-permute-start | bytes 589832 | tf_op jit(solution)/shard_map/ppermute | solution.py:13
  142.6 9.6 %collective-permute-start.16 = (bf16[32,3072]{1,0:T(8,128)(2,1)}, bf16[32,3072]{1,0:T(8,128)(2,1)}, u32[]{:S(2)}, u32[]{:S(2)}) collective-permute-start(bf16[32,3072]{1,0:T(8,128)(2,1)} %get-tuple-element.23), channel_id=1, source_target_pairs={{0,2},{1,3},{2,0},{3,1},{4,6},{5,7},{6,4},{7,5},{8,10},{9,11},{10,... | collective-permute-start | bytes 589832 | tf_op jit(solution)/shard_map/ppermute | solution.py:13
  158.8 20.4 %all-to-all-start.1 = ((bf16[16,4,3072]{2,1,0:T(4,128)(2,1)}), bf16[16,4,3072]{2,1,0:T(4,128)(2,1)S(1)}, u32[]{:S(2)}, u32[]{:S(2)}) async-start(bf16[16,4,3072]{2,1,0:T(4,128)(2,1)} %bitcast.73), calls=%async_computation.1 | async-start | bytes 786432 | tf_op jit(solution)/shard_map/all_to_all | solution.py:95
  (17 other events, 400.8 us)

commit v2 on v1

v2 whole, which is shorter than its diff:
```python
import jax
import jax.numpy as jnp
from jax import lax
from jax.sharding import Mesh, PartitionSpec as P

BF = jnp.bfloat16
F32 = jnp.float32
Z = ("zh", "zl")
SLAB = ("core", "y", "x")
SIDE = 4


def hop(value, order, step):
    pairs = []
    for core in range(2):
        for y in range(SIDE):
            for x in range(SIDE):
                to_y, to_x = (y, (x + step) % SIDE) if core == order else ((y + step) % SIDE, x)
                pairs.append(((core * SIDE + y) * SIDE + x, (core * SIDE + to_y) * SIDE + to_x))
    return lax.ppermute(value, SLAB, pairs)


def swap(value):
    return lax.ppermute(value, "core", [(0, 1), (1, 0)])


def rank_slots(flat_routes):
    count = flat_routes.shape[0]
    positions = jnp.arange(count, dtype=jnp.int32)
    before = positions[:, None] < positions[None, :]
    matches = flat_routes[:, None] == flat_routes[None, :]
    return jnp.sum(jnp.logical_and(matches, before), axis=0)


def exact(choice, value):
    return jnp.dot(choice.astype(BF), value, preferred_element_type=F32)


def expert_rows(grad_rows, gate_mat, up_mat, down_mat, pre_gate, pre_up):
    contract = (((1,), (1,)), ((), ()))
    hidden_grad = lax.dot_general(grad_rows, down_mat, contract, preferred_element_type=F32)
    gate_vals = pre_gate.astype(F32)
    up_vals = pre_up.astype(F32)
    sigmoid_gate = jax.nn.sigmoid(gate_vals)
    up_grad = (hidden_grad * gate_vals * sigmoid_gate).astype(BF)
    gate_grad = (
        hidden_grad * up_vals * sigmoid_gate * (1.0 + gate_vals * (1.0 - sigmoid_gate))
    ).astype(BF)
    partial_value = lax.dot_general(gate_grad, gate_mat, contract, preferred_element_type=F32)
    partial_value += lax.dot_general(up_grad, up_mat, contract, preferred_element_type=F32)
    return partial_value.astype(BF)


def shards(out_grad, routes, gate_weight, gate_proj, up_proj, down_proj, saved_gate, saved_up):
    tok, dim = out_grad.shape
    my_x, my_y = lax.axis_index("x"), lax.axis_index("y")
    core = lax.axis_index("core")

    flat_routes = routes.reshape(-1)
    slot = rank_slots(flat_routes)
    key = ((flat_routes // 2) * 2 + (flat_routes + core) % 2) * 4 + slot
    key = key.reshape(tok, 2)
    places = jnp.arange(64, dtype=jnp.int32)
    place_key = ((places // 16) * 2 + (places // 4) % 2) * 4 + places % 4
    match = place_key[:, None, None] == key[None, :, :]
    weight = jnp.sum(jnp.where(match, gate_weight[None], 0.0), axis=(1, 2))
    chosen = jnp.any(match, axis=2)
    outgoing = (exact(chosen, out_grad) * weight[:, None]).astype(BF)
    arrived = lax.all_to_all(outgoing, Z, split_axis=0, concat_axis=0, tiled=True)
    turned = (places % 32) // 4 * 8 + places // 32 * 4 + places % 4
    turn = turned[:, None] == places[None, :]
    own = exact(turn, arrived).astype(BF)

    def saved_rows(group):
        count = len(group) * 256
        i = jnp.arange(count, dtype=jnp.int32)
        outer = jnp.asarray(group, jnp.int32)[i // 256]
        source = (core + (i // 128) % 2) % 2
        inner = jnp.asarray((0, 3, 1, 2), jnp.int32)[(i // 32) % 4]
        step_y = jnp.where(source == 0, outer, inner)
        step_x = jnp.where(source == 0, inner, outer)
        z = (i // 4) % 8
        block = ((my_y + step_y) % 4 * 2 + z % 2) * 4 + (my_x + step_x) % 4
        row = block * 32 + ((z // 2) * 2 + source) * 4 + i % 4
        choice = row[:, None] == jnp.arange(saved_gate.shape[1], dtype=jnp.int32)[None, :]
        return exact(choice, saved_gate[0]).astype(BF), exact(choice, saved_up[0]).astype(BF)

    pre = (saved_rows((3, 1)), saved_rows((2,)), saved_rows((0,)))
    own, pre = lax.optimization_barrier((own, pre))
    pre_sides, pre_end, pre_line = pre

    before, after = hop(own, 0, 1), hop(own, 0, -1)
    far = hop(before, 0, 1)
    ring = (own, before, after, far)
    line = [jnp.concatenate([v[k * 32:k * 32 + 32] for v in ring], 0) for k in (0, 1)]
    weights = (gate_proj[0], up_proj[0], down_proj[0])
    line_other = swap(line[1])
    back0, ahead1 = hop(line[0], 1, 1), hop(line[1], 1, -1)
    line, line_other = lax.optimization_barrier((line, line_other))
    back1, ahead0 = hop(line[1], 1, 1), hop(line[0], 1, -1)
    end0, end1 = hop(back0, 1, 1), hop(ahead1, 1, -1)
    ahead_other, back_other = swap(ahead1), swap(back1)
    end_other = swap(end1)
    middle = expert_rows(jnp.concatenate([line[0], line_other], 0), *weights, *pre_line)
    middle, back_other, ahead0 = lax.optimization_barrier((middle, back_other, ahead0))
    sides = expert_rows(
        jnp.concatenate([back0, back_other, ahead0, ahead_other], 0), *weights, *pre_sides
    )
    to_back0, to_back1, to_ahead0, to_ahead1 = [sides[k * 128:k * 128 + 128] for k in range(4)]
    to_back1, to_ahead1 = swap(to_back1), swap(to_ahead1)
    got_ahead1, got_back0 = hop(to_back1, 1, -1), hop(to_ahead0, 1, 1)
    sides, end0, end_other = lax.optimization_barrier((sides, end0, end_other))
    ends = expert_rows(jnp.concatenate([end0, end_other], 0), *weights, *pre_end)
    far0, far1 = hop(ends[:128], 1, -1), hop(swap(ends[128:]), 1, 1)
    middle0, middle1 = middle[:128], swap(middle[128:])
    got_ahead0 = hop((to_back0.astype(F32) + far0.astype(F32)).astype(BF), 1, -1)
    got_back1 = hop((to_ahead1.astype(F32) + far1.astype(F32)).astype(BF), 1, 1)

    def add(*values):
        return sum(v.astype(F32) for v in values)

    sums = [add(middle0, got_back0, got_ahead0), add(middle1, got_back1, got_ahead1)]
    mine, to_before, to_after, to_far = [
        jnp.concatenate([s[k * 32:k * 32 + 32] for s in sums], 0) for k in range(4)
    ]
    passed = hop(to_far.astype(BF), 0, -1)
    got_before = hop(to_after.astype(BF), 0, 1)
    got_after = hop(add(to_before, passed).astype(BF), 0, -1)
    total = add(mine, got_before, got_after).astype(BF)
    turn_back = turned[None, :] == places[:, None]
    total = exact(turn_back, total).astype(BF)
    returned = lax.all_to_all(total, Z, split_axis=0, concat_axis=0, tiled=True)
    return exact(chosen.T, returned).astype(BF)


def solution(mesh):
    fine = Mesh(mesh.devices.reshape(4, 2, 4, 2, 4), ("zh", "core", "y", "zl", "x"))
    expert, cuts = ("zh", "core"), ("y", "zl", "x")
    rows = P(expert + cuts, None)
    in_specs = (
        rows,
        rows,
        rows,
        P(expert, None, cuts),
        P(expert, None, cuts),
        P(expert, cuts, None),
        P(expert, None, cuts),
        P(expert, None, cuts),
    )
    return jax.shard_map(shards, mesh=fine, in_specs=in_specs, out_specs=rows, check_vma=False)
```

time: 184 us -> 156 us (0.85)
  local copies, waits for them, and re-layouts: 18.7 us -> 1.82 us
  blocking collectives: 0 us -> 14.9 us
  starting transfers between devices: 48.9 us -> 35.1 us
  waiting for transfers between devices: 86.1 us -> 74.4 us
  matrix products: 15.1 us -> 25.9 us
  other arithmetic: 12.4 us -> 2.44 us
    all_to_all x0 -> x1, blocking collectives: none -> 14.9 us  [shards(): returned = lax.all_to_all(total, Z, split_axis=0, concat_axis=0, tiled=True)]
    dot_general x2 -> x10, matrix products: 3.01 us -> 13.7 us  [exact(): return jnp.dot(choice.astype(BF), value, preferred_element_type=F32)]
    all_to_all x2 -> x1, waiting for transfers between devices: 14.1 us -> 3.99 us  [shards(): lax.all_to_all(outgoing, Z, split_axis=0, concat_axis=0, tiled=True)]
    all_to_all x2 -> x1, starting transfers between devices: 16.3 us -> 8.46 us  [shards(): lax.all_to_all(outgoing, Z, split_axis=0, concat_axis=0, tiled=True)]
    concatenate x3 -> x4, other arithmetic: 7.49 us -> 0.16 us  [the longest x2 0.11 us: shards(): jnp.concatenate([v[k * 32:k * 32 + 32] for v in ring], 0)]
    unnamed x43 -> x23, local copies, waits for them, and re-layouts: 7.41 us -> 0.96 us
    ppermute x24 -> x26, starting transfers between devices: 32.7 us -> 26.6 us  [the longest x18 25.2 us: hop(): return lax.ppermute(value, SLAB, pairs)]
    slice x13 -> x9, local copies, waits for them, and re-layouts: 5 us -> 0.61 us  [the longest x2 0.2 us: shards(): s[k * 32:k * 32 + 32]]
  transfers between devices with their start and end apart: 26 -> 27, of which waited for: 15 -> 14; matrix products, arithmetic and copies ran while one was open for 16% -> 13% of each run, Pallas kernels for 0% -> 0%
where the time goes in v2:
time: 156 us; the launch traced here: 155 us
  waiting for transfers between devices  74.4 us (48%)
  starting transfers between devices  35.1 us (22%)
  matrix products  25.9 us (17%)
  blocking collectives  14.9 us (10%)
  other arithmetic  2.44 us (2%)
  local copies, waits for them, and re-layouts  1.82 us (1%)
    ppermute x18, waiting for transfers between devices, hop(): return lax.ppermute(value, SLAB, pairs)  69.2 us
    ppermute x18, starting transfers between devices, hop(): return lax.ppermute(value, SLAB, pairs)  25.2 us
    all_to_all x1, blocking collectives, shards(): returned = lax.all_to_all(total, Z, split_axis=0, concat_axis=0, tiled=True)  14.9 us
    dot_general x10, matrix products, exact(): return jnp.dot(choice.astype(BF), value, preferred_element_type=F32)  13.7 us
    all_to_all x1, starting transfers between devices, shards(): lax.all_to_all(outgoing, Z, split_axis=0, concat_axis=0, tiled=True)  8.46 us
    dot_general x3, matrix products, expert_rows(): lax.dot_general(gate_grad, gate_mat, contract, preferred_element_type=F32)  4.26 us
    dot_general x3, matrix products, expert_rows(): lax.dot_general(up_grad, up_mat, contract, preferred_element_type=F32)  4.08 us
    all_to_all x1, waiting for transfers between devices, shards(): lax.all_to_all(outgoing, Z, split_axis=0, concat_axis=0, tiled=True)  3.99 us
  transfers between devices with their start and end apart: 27, of which 14 were waited for; matrix products, arithmetic and copies ran while one was open for 13% of the time, Pallas kernels for 0%

profile of v2, /device:TPU:24, one launch (start us, length us, event | category | flops | bytes accessed | tf_op | source)
XLA Modules:
  0.0 155.1 jit_solution(9646750401290553415)
XLA Ops:
  4.0 8.5 %all-to-all-start = ((bf16[8,8,3072]{2,1,0:T(8,128)(2,1)}), bf16[8,8,3072]{2,1,0:T(8,128)(2,1)S(1)}, u32[]{:S(2)}, u32[]{:S(2)}) async-start(bf16[8,8,3072]{2,1,0:T(8,128)(2,1)} %fusion.3), calls=%async_computation | async-start | bytes 786432 | tf_op jit(solution)/shard_map/all_to_all | solution.py:69
  12.5 2.6 %convolution_convert_fusion.3 = bf16[256,512]{1,0:T(8,128)(2,1)} fusion(bf16[1,1024,512]{2,1,0:T(8,128)(2,1)} %param.21, s32[256]{0:T(256)S(1)} %get-tuple-element.60), kind=kOutput, calls=%fused_computation.52 | convolution fusion | flops 268828672 | bytes 1311744 | tf_op jit(solution)/shard_map/dot_general | solution.py:36
  15.1 2.4 %convolution_convert_fusion.4 = bf16[256,512]{1,0:T(8,128)(2,1)} fusion(bf16[1,1024,512]{2,1,0:T(8,128)(2,1)} %param.20, s32[256]{0:T(256)S(1)} %get-tuple-element.60), kind=kOutput, calls=%fused_computation.53 | convolution fusion | flops 268828672 | bytes 1311744 | tf_op jit(solution)/shard_map/dot_general | solution.py:36
  23.1 4.0 %all-to-all-done = bf16[8,8,3072]{2,1,0:T(8,128)(2,1)S(1)} async-done(((bf16[8,8,3072]{2,1,0:T(8,128)(2,1)}), bf16[8,8,3072]{2,1,0:T(8,128)(2,1)S(1)}, u32[]{:S(2)}, u32[]{:S(2)}) %all-to-all-start) | async-done | bytes 393248 | tf_op jit(solution)/shard_map/all_to_all | solution.py:69
  30.8 5.7 %collective-permute-done = bf16[64,3072]{1,0:T(8,128)(2,1)S(1)} collective-permute-done((bf16[64,3072]{1,0:T(8,128)(2,1)S(1)}, bf16[64,3072]{1,0:T(8,128)(2,1)S(1)}, u32[]{:S(2)}, u32[]{:S(2)}) %collective-permute-start) | collective-permute-done | bytes 393248 | tf_op jit(solution)/shard_map/ppermute | solution.py:20
  36.9 8.6 %collective-permute-done.2 = bf16[64,3072]{1,0:T(8,128)(2,1)S(1)} collective-permute-done((bf16[64,3072]{1,0:T(8,128)(2,1)S(1)}, bf16[64,3072]{1,0:T(8,128)(2,1)S(1)}, u32[]{:S(2)}, u32[]{:S(2)}) %collective-permute-start.2) | collective-permute-done | bytes 393248 | tf_op jit(solution)/shard_map/ppermute | solution.py:20
  46.6 2.6 %collective-permute-start.7 = (bf16[128,3072]{1,0:T(8,128)(2,1)S(1)}, bf16[128,3072]{1,0:T(8,128)(2,1)S(1)}, u32[]{:S(2)}, u32[]{:S(2)}) collective-permute-start(bf16[128,3072]{1,0:T(8,128)(2,1)S(1)} %pad_maximum_fusion), channel_id=1, source_target_pairs={{0,8},{1,9},{2,10},{3,11},{8,16},{9,17},{10,18},{11,19},{16,24},{1... | collective-permute-start | bytes 2359304 | tf_op jit(solution)/shard_map/ppermute | solution.py:20
  49.3 1.9 %collective-permute-start.6 = (bf16[128,3072]{1,0:T(8,128)(2,1)S(1)}, bf16[128,3072]{1,0:T(8,128)(2,1)S(1)}, u32[]{:S(2)}, u32[]{:S(2)}) collective-permute-start(bf16[128,3072]{1,0:T(8,128)(2,1)S(1)} %pad_maximum_fusion), channel_id=1, source_target_pairs={{0,24},{1,25},{2,26},{3,27},{8,0},{9,1},{10,2},{11,3},{16,8},{17,9... | collective-permute-start | bytes 2359304 | tf_op jit(solution)/shard_map/ppermute | solution.py:20
  51.2 7.8 %collective-permute-done.8 = bf16[128,3072]{1,0:T(8,128)(2,1)S(1)} collective-permute-done((bf16[128,3072]{1,0:T(8,128)(2,1)S(1)}, bf16[128,3072]{1,0:T(8,128)(2,1)S(1)}, u32[]{:S(2)}, u32[]{:S(2)}) %collective-permute-start.8) | collective-permute-done | bytes 786464 | tf_op jit(solution)/shard_map/ppermute | solution.py:20
  59.0 3.4 %collective-permute-start.11 = (bf16[128,3072]{1,0:T(8,128)(2,1)S(1)}, bf16[128,3072]{1,0:T(8,128)(2,1)S(1)}, u32[]{:S(2)}, u32[]{:S(2)}) collective-permute-start(bf16[128,3072]{1,0:T(8,128)(2,1)S(1)} %collective-permute-done.7), channel_id=1, source_target_pairs={{0,8},{1,9},{2,10},{3,11},{8,16},{9,17},{10,18},{11,19},{16,24},{1... | collective-permute-start | bytes 2359304 | tf_op jit(solution)/shard_map/ppermute | solution.py:20
  63.4 3.7 %collective-permute-done.4 = bf16[128,3072]{1,0:T(8,128)(2,1)S(1)} collective-permute-done((bf16[128,3072]{1,0:T(8,128)(2,1)S(1)}, bf16[128,3072]{1,0:T(8,128)(2,1)S(1)}, u32[]{:S(2)}, u32[]{:S(2)}) %collective-permute-start.4) | collective-permute-done | bytes 786464 | tf_op jit(solution)/shard_map/ppermute | solution.py:20
  69.4 6.4 %collective-permute-done.12 = bf16[128,3072]{1,0:T(8,128)(2,1)S(1)} collective-permute-done((bf16[128,3072]{1,0:T(8,128)(2,1)S(1)}, bf16[128,3072]{1,0:T(8,128)(2,1)S(1)}, u32[]{:S(2)}, u32[]{:S(2)}) %collective-permute-start.12) | collective-permute-done | bytes 786464 | tf_op jit(solution)/shard_map/ppermute | solution.py:20
  77.7 2.0 %fusion.18 = f32[512,3072]{1,0:T(8,128)S(1)} fusion(bf16[1,3072,512]{2,1,0:T(8,128)(2,1)S(1)} %copy-done, bf16[512,512]{1,0:T(8,128)(2,1)S(1)} %copy-done.4, f32[512,512]{1,0:T(8,128)S(1)} %fusion.5, bf16[512,512]{1,0:T(8,128)(2,1)S(1)} %copy-done.10), kind=kOutput, calls=%fused_computation.25 | convolution fusion | flops 1613758464 | bytes 11534336 | tf_op jit(solution)/shard_map/dot_general | solution.py:49
  87.5 2.1 %collective-permute-start.19 = (bf16[128,3072]{1,0:T(8,128)(2,1)S(1)}, bf16[128,3072]{1,0:T(8,128)(2,1)S(1)}, u32[]{:S(2)}, u32[]{:S(2)}) collective-permute-start(bf16[128,3072]{1,0:T(8,128)(2,1)S(1)} %collective-permute-done.18), channel_id=1, source_target_pairs={{0,8},{1,9},{2,10},{3,11},{8,16},{9,17},{10,18},{11,19},{16,24},{1... | collective-permute-start | bytes 2359304 | tf_op jit(solution)/shard_map/ppermute | solution.py:20
  89.7 9.2 %collective-permute-done.14 = bf16[128,3072]{1,0:T(8,128)(2,1)S(1)} collective-permute-done((bf16[128,3072]{1,0:T(8,128)(2,1)S(1)}, bf16[128,3072]{1,0:T(8,128)(2,1)S(1)}, u32[]{:S(2)}, u32[]{:S(2)}) %collective-permute-start.14) | collective-permute-done | bytes 786464 | tf_op jit(solution)/shard_map/ppermute | solution.py:20
  99.7 3.4 %collective-permute-start.20 = (bf16[128,3072]{1,0:T(8,128)(2,1)S(1)}, bf16[128,3072]{1,0:T(8,128)(2,1)S(1)}, u32[]{:S(2)}, u32[]{:S(2)}) collective-permute-start(bf16[128,3072]{1,0:T(8,128)(2,1)S(1)} %add_convert_fusion.1), channel_id=1, source_target_pairs={{0,8},{1,9},{2,10},{3,11},{8,16},{9,17},{10,18},{11,19},{16,24},{1... | collective-permute-start | bytes 2359304 | tf_op jit(solution)/shard_map/ppermute | solution.py:20
  103.1 4.9 %collective-permute-done.10 = bf16[128,3072]{1,0:T(8,128)(2,1)S(1)} collective-permute-done((bf16[128,3072]{1,0:T(8,128)(2,1)S(1)}, bf16[128,3072]{1,0:T(8,128)(2,1)S(1)}, u32[]{:S(2)}, u32[]{:S(2)}) %collective-permute-start.10) | collective-permute-done | bytes 786464 | tf_op jit(solution)/shard_map/ppermute | solution.py:20
  108.0 4.3 %collective-permute-done.15 = bf16[128,3072]{1,0:T(8,128)(2,1)S(1)} collective-permute-done((bf16[128,3072]{1,0:T(8,128)(2,1)S(1)}, bf16[128,3072]{1,0:T(8,128)(2,1)S(1)}, u32[]{:S(2)}, u32[]{:S(2)}) %collective-permute-start.15) | collective-permute-done | bytes 786464 | tf_op jit(solution)/shard_map/ppermute | solution.py:20
  112.7 8.0 %collective-permute-done.22 = bf16[128,3072]{1,0:T(8,128)(2,1)S(1)} collective-permute-done((bf16[128,3072]{1,0:T(8,128)(2,1)S(1)}, bf16[128,3072]{1,0:T(8,128)(2,1)S(1)}, u32[]{:S(2)}, u32[]{:S(2)}) %collective-permute-start.22) | collective-permute-done | bytes 786464 | tf_op jit(solution)/shard_map/ppermute | solution.py:20
  121.4 3.3 %collective-permute-start.24 = (bf16[64,3072]{1,0:T(8,128)(2,1)S(1)}, bf16[64,3072]{1,0:T(8,128)(2,1)S(1)}, u32[]{:S(2)}, u32[]{:S(2)}) collective-permute-start(bf16[64,3072]{1,0:T(8,128)(2,1)S(1)} %pad_maximum_fusion.3), channel_id=1, source_target_pairs={{0,3},{1,0},{2,1},{3,2},{8,11},{9,8},{10,9},{11,10},{16,19},{17,16... | collective-permute-start | bytes 1179656 | tf_op jit(solution)/shard_map/ppermute | solution.py:20
  124.8 5.2 %collective-permute-done.24 = bf16[64,3072]{1,0:T(8,128)(2,1)S(1)} collective-permute-done((bf16[64,3072]{1,0:T(8,128)(2,1)S(1)}, bf16[64,3072]{1,0:T(8,128)(2,1)S(1)}, u32[]{:S(2)}, u32[]{:S(2)}) %collective-permute-start.24) | collective-permute-done | bytes 393248 | tf_op jit(solution)/shard_map/ppermute | solution.py:20
  130.0 3.8 %collective-permute-start.25 = (bf16[64,3072]{1,0:T(8,128)(2,1)S(1)}, bf16[64,3072]{1,0:T(8,128)(2,1)S(1)}, u32[]{:S(2)}, u32[]{:S(2)}) collective-permute-start(bf16[64,3072]{1,0:T(8,128)(2,1)S(1)} %fusion.55), channel_id=1, source_target_pairs={{0,3},{1,0},{2,1},{3,2},{8,11},{9,8},{10,9},{11,10},{16,19},{17,16... | collective-permute-start | bytes 1179656 | tf_op jit(solution)/shard_map/ppermute | solution.py:20
  133.8 5.3 %collective-permute-done.25 = bf16[64,3072]{1,0:T(8,128)(2,1)S(1)} collective-permute-done((bf16[64,3072]{1,0:T(8,128)(2,1)S(1)}, bf16[64,3072]{1,0:T(8,128)(2,1)S(1)}, u32[]{:S(2)}, u32[]{:S(2)}) %collective-permute-start.25) | collective-permute-done | bytes 393248 | tf_op jit(solution)/shard_map/ppermute | solution.py:20
  139.4 14.9 %all_to_all.24 = bf16[8,8,3072]{2,1,0:T(8,128)(2,1)S(1)} all-to-all(bf16[8,8,3072]{2,1,0:T(8,128)(2,1)S(1)} %fusion.4), channel_id=1, replica_groups=mesh['zh'=4,'core'=2,'y'=4,'zl'=2,'x'=4] {'zh','zl'}, dimensions={0} | all-to-all | bytes 786432 | tf_op jit(solution)/shard_map/all_to_all | solution.py:132
  (105 shorter events, 30.7 us)
Async XLA Ops:
  4.0 23.1 %all-to-all-start = ((bf16[8,8,3072]{2,1,0:T(8,128)(2,1)}), bf16[8,8,3072]{2,1,0:T(8,128)(2,1)S(1)}, u32[]{:S(2)}, u32[]{:S(2)}) async-start(bf16[8,8,3072]{2,1,0:T(8,128)(2,1)} %fusion.3), calls=%async_computation | async-start | bytes 786432 | tf_op jit(solution)/shard_map/all_to_all | solution.py:69
  27.5 9.1 %collective-permute-start = (bf16[64,3072]{1,0:T(8,128)(2,1)S(1)}, bf16[64,3072]{1,0:T(8,128)(2,1)S(1)}, u32[]{:S(2)}, u32[]{:S(2)}) collective-permute-start(bf16[64,3072]{1,0:T(8,128)(2,1)S(1)} %convolution_convert_fusion.1), channel_id=1, source_target_pairs={{0,1},{1,2},{2,3},{3,0},{8,9},{9,10},{10,11},{11,8},{16,17},{17,18... | collective-permute-start | bytes 1179656 | tf_op jit(solution)/shard_map/ppermute | solution.py:20
  29.0 7.8 %collective-permute-start.1 = (bf16[64,3072]{1,0:T(8,128)(2,1)S(1)}, bf16[64,3072]{1,0:T(8,128)(2,1)S(1)}, u32[]{:S(2)}, u32[]{:S(2)}) collective-permute-start(bf16[64,3072]{1,0:T(8,128)(2,1)S(1)} %convolution_convert_fusion.1), channel_id=1, source_target_pairs={{0,3},{1,0},{2,1},{3,2},{8,11},{9,8},{10,9},{11,10},{16,19},{17,16... | collective-permute-start | bytes 1179656 | tf_op jit(solution)/shard_map/ppermute | solution.py:20
  36.5 9.0 %collective-permute-start.2 = (bf16[64,3072]{1,0:T(8,128)(2,1)S(1)}, bf16[64,3072]{1,0:T(8,128)(2,1)S(1)}, u32[]{:S(2)}, u32[]{:S(2)}) collective-permute-start(bf16[64,3072]{1,0:T(8,128)(2,1)S(1)} %collective-permute-done), channel_id=1, source_target_pairs={{0,1},{1,2},{2,3},{3,0},{8,9},{9,10},{10,11},{11,8},{16,17},{17,18... | collective-permute-start | bytes 1179656 | tf_op jit(solution)/shard_map/ppermute | solution.py:20
  45.7 13.3 %collective-permute-start.8 = (bf16[128,3072]{1,0:T(8,128)(2,1)S(1)}, bf16[128,3072]{1,0:T(8,128)(2,1)S(1)}, u32[]{:S(2)}, u32[]{:S(2)}) collective-permute-start(bf16[128,3072]{1,0:T(8,128)(2,1)S(1)} %pad_maximum_fusion.1), channel_id=1, source_target_pairs={{0,24},{1,25},{2,26},{3,27},{8,0},{9,1},{10,2},{11,3},{16,8},{17,9... | collective-permute-start | bytes 2359304 | tf_op jit(solution)/shard_map/ppermute | solution.py:20
  46.6 12.4 %collective-permute-start.7 = (bf16[128,3072]{1,0:T(8,128)(2,1)S(1)}, bf16[128,3072]{1,0:T(8,128)(2,1)S(1)}, u32[]{:S(2)}, u32[]{:S(2)}) collective-permute-start(bf16[128,3072]{1,0:T(8,128)(2,1)S(1)} %pad_maximum_fusion), channel_id=1, source_target_pairs={{0,8},{1,9},{2,10},{3,11},{8,16},{9,17},{10,18},{11,19},{16,24},{1... | collective-permute-start | bytes 2359304 | tf_op jit(solution)/shard_map/ppermute | solution.py:20
  49.2 17.9 %collective-permute-start.4 = (bf16[128,3072]{1,0:T(8,128)(2,1)S(1)}, bf16[128,3072]{1,0:T(8,128)(2,1)S(1)}, u32[]{:S(2)}, u32[]{:S(2)}) collective-permute-start(bf16[128,3072]{1,0:T(8,128)(2,1)S(1)} %pad_maximum_fusion.1), channel_id=1, source_target_pairs={{0,8},{1,9},{2,10},{3,11},{8,16},{9,17},{10,18},{11,19},{16,24},{1... | collective-permute-start | bytes 2359304 | tf_op jit(solution)/shard_map/ppermute | solution.py:20
  49.3 26.6 %collective-permute-start.6 = (bf16[128,3072]{1,0:T(8,128)(2,1)S(1)}, bf16[128,3072]{1,0:T(8,128)(2,1)S(1)}, u32[]{:S(2)}, u32[]{:S(2)}) collective-permute-start(bf16[128,3072]{1,0:T(8,128)(2,1)S(1)} %pad_maximum_fusion), channel_id=1, source_target_pairs={{0,24},{1,25},{2,26},{3,27},{8,0},{9,1},{10,2},{11,3},{16,8},{17,9... | collective-permute-start | bytes 2359304 | tf_op jit(solution)/shard_map/ppermute | solution.py:20
  59.0 16.9 %collective-permute-start.9 = (bf16[128,3072]{1,0:T(8,128)(2,1)S(1)}, bf16[128,3072]{1,0:T(8,128)(2,1)S(1)}, u32[]{:S(2)}, u32[]{:S(2)}) collective-permute-start(bf16[128,3072]{1,0:T(8,128)(2,1)S(1)} %collective-permute-done.8), channel_id=1, source_target_pairs={{0,32},{32,0},{1,33},{33,1},{2,34},{34,2},{3,35},{35,3},{4,36},{36... | collective-permute-start | bytes 2359304 | tf_op jit(solution)/shard_map/ppermute | solution.py:24
  59.0 16.8 %collective-permute-start.12 = (bf16[128,3072]{1,0:T(8,128)(2,1)S(1)}, bf16[128,3072]{1,0:T(8,128)(2,1)S(1)}, u32[]{:S(2)}, u32[]{:S(2)}) collective-permute-start(bf16[128,3072]{1,0:T(8,128)(2,1)S(1)} %collective-permute-done.8), channel_id=1, source_target_pairs={{0,24},{1,25},{2,26},{3,27},{8,0},{9,1},{10,2},{11,3},{16,8},{17,9... | collective-permute-start | bytes 2359304 | tf_op jit(solution)/shard_map/ppermute | solution.py:20
  59.0 22.7 %collective-permute-start.11 = (bf16[128,3072]{1,0:T(8,128)(2,1)S(1)}, bf16[128,3072]{1,0:T(8,128)(2,1)S(1)}, u32[]{:S(2)}, u32[]{:S(2)}) collective-permute-start(bf16[128,3072]{1,0:T(8,128)(2,1)S(1)} %collective-permute-done.7), channel_id=1, source_target_pairs={{0,8},{1,9},{2,10},{3,11},{8,16},{9,17},{10,18},{11,19},{16,24},{1... | collective-permute-start | bytes 2359304 | tf_op jit(solution)/shard_map/ppermute | solution.py:20
  67.1 8.7 %collective-permute-start.5 = (bf16[128,3072]{1,0:T(8,128)(2,1)S(1)}, bf16[128,3072]{1,0:T(8,128)(2,1)S(1)}, u32[]{:S(2)}, u32[]{:S(2)}) collective-permute-start(bf16[128,3072]{1,0:T(8,128)(2,1)S(1)} %collective-permute-done.4), channel_id=1, source_target_pairs={{0,32},{32,0},{1,33},{33,1},{2,34},{34,2},{3,35},{35,3},{4,36},{36... | collective-permute-start | bytes 2359304 | tf_op jit(solution)/shard_map/ppermute | solution.py:24
  85.6 13.2 %collective-permute-start.14 = (bf16[128,3072]{1,0:T(8,128)(2,1)S(1)}, bf16[128,3072]{1,0:T(8,128)(2,1)S(1)}, u32[]{:S(2)}, u32[]{:S(2)}) collective-permute-start(bf16[128,3072]{1,0:T(8,128)(2,1)S(1)} %get-tuple-element.46), channel_id=1, source_target_pairs={{0,24},{1,25},{2,26},{3,27},{8,0},{9,1},{10,2},{11,3},{16,8},{17,9... | collective-permute-start | bytes 2359304 | tf_op jit(solution)/shard_map/ppermute | solution.py:20
  85.8 13.4 %collective-permute-start.17 = (bf16[128,3072]{1,0:T(8,128)(2,1)S(1)}, bf16[128,3072]{1,0:T(8,128)(2,1)S(1)}, u32[]{:S(2)}, u32[]{:S(2)}) collective-permute-start(bf16[128,3072]{1,0:T(8,128)(2,1)S(1)} %get-tuple-element.41), channel_id=1, source_target_pairs={{0,32},{32,0},{1,33},{33,1},{2,34},{34,2},{3,35},{35,3},{4,36},{36... | collective-permute-start | bytes 2359304 | tf_op jit(solution)/shard_map/ppermute | solution.py:24
  86.2 13.1 %collective-permute-start.21 = (bf16[128,3072]{1,0:T(8,128)(2,1)S(1)}, bf16[128,3072]{1,0:T(8,128)(2,1)S(1)}, u32[]{:S(2)}, u32[]{:S(2)}) collective-permute-start(bf16[128,3072]{1,0:T(8,128)(2,1)S(1)} %get-tuple-element.40), channel_id=1, source_target_pairs={{0,32},{32,0},{1,33},{33,1},{2,34},{34,2},{3,35},{35,3},{4,36},{36... | collective-permute-start | bytes 2359304 | tf_op jit(solution)/shard_map/ppermute | solution.py:24
  87.5 12.0 %collective-permute-start.19 = (bf16[128,3072]{1,0:T(8,128)(2,1)S(1)}, bf16[128,3072]{1,0:T(8,128)(2,1)S(1)}, u32[]{:S(2)}, u32[]{:S(2)}) collective-permute-start(bf16[128,3072]{1,0:T(8,128)(2,1)S(1)} %collective-permute-done.18), channel_id=1, source_target_pairs={{0,8},{1,9},{2,10},{3,11},{8,16},{9,17},{10,18},{11,19},{16,24},{1... | collective-permute-start | bytes 2359304 | tf_op jit(solution)/shard_map/ppermute | solution.py:20
  89.6 18.3 %collective-permute-start.10 = (bf16[128,3072]{1,0:T(8,128)(2,1)S(1)}, bf16[128,3072]{1,0:T(8,128)(2,1)S(1)}, u32[]{:S(2)}, u32[]{:S(2)}) collective-permute-start(bf16[128,3072]{1,0:T(8,128)(2,1)S(1)} %get-tuple-element.39), channel_id=1, source_target_pairs={{0,8},{1,9},{2,10},{3,11},{8,16},{9,17},{10,18},{11,19},{16,24},{1... | collective-permute-start | bytes 2359304 | tf_op jit(solution)/shard_map/ppermute | solution.py:20
  99.0 13.3 %collective-permute-start.15 = (bf16[128,3072]{1,0:T(8,128)(2,1)S(1)}, bf16[128,3072]{1,0:T(8,128)(2,1)S(1)}, u32[]{:S(2)}, u32[]{:S(2)}) collective-permute-start(bf16[128,3072]{1,0:T(8,128)(2,1)S(1)} %add_convert_fusion.2), channel_id=1, source_target_pairs={{0,24},{1,25},{2,26},{3,27},{8,0},{9,1},{10,2},{11,3},{16,8},{17,9... | collective-permute-start | bytes 2359304 | tf_op jit(solution)/shard_map/ppermute | solution.py:20
  99.2 13.5 %collective-permute-start.16 = (bf16[128,3072]{1,0:T(8,128)(2,1)S(1)}, bf16[128,3072]{1,0:T(8,128)(2,1)S(1)}, u32[]{:S(2)}, u32[]{:S(2)}) collective-permute-start(bf16[128,3072]{1,0:T(8,128)(2,1)S(1)} %slice.89), channel_id=1, source_target_pairs={{0,32},{32,0},{1,33},{33,1},{2,34},{34,2},{3,35},{35,3},{4,36},{36... | collective-permute-start | bytes 2359304 | tf_op jit(solution)/shard_map/ppermute | solution.py:24
  99.3 21.4 %collective-permute-start.22 = (bf16[128,3072]{1,0:T(8,128)(2,1)S(1)}, bf16[128,3072]{1,0:T(8,128)(2,1)S(1)}, u32[]{:S(2)}, u32[]{:S(2)}) collective-permute-start(bf16[128,3072]{1,0:T(8,128)(2,1)S(1)} %collective-permute-done.21), channel_id=1, source_target_pairs={{0,24},{1,25},{2,26},{3,27},{8,0},{9,1},{10,2},{11,3},{16,8},{17,9... | collective-permute-start | bytes 2359304 | tf_op jit(solution)/shard_map/ppermute | solution.py:20
  99.7 21.0 %collective-permute-start.20 = (bf16[128,3072]{1,0:T(8,128)(2,1)S(1)}, bf16[128,3072]{1,0:T(8,128)(2,1)S(1)}, u32[]{:S(2)}, u32[]{:S(2)}) collective-permute-start(bf16[128,3072]{1,0:T(8,128)(2,1)S(1)} %add_convert_fusion.1), channel_id=1, source_target_pairs={{0,8},{1,9},{2,10},{3,11},{8,16},{9,17},{10,18},{11,19},{16,24},{1... | collective-permute-start | bytes 2359304 | tf_op jit(solution)/shard_map/ppermute | solution.py:20
  121.2 12.6 %collective-permute-start.23 = (bf16[64,3072]{1,0:T(8,128)(2,1)S(1)}, bf16[64,3072]{1,0:T(8,128)(2,1)S(1)}, u32[]{:S(2)}, u32[]{:S(2)}) collective-permute-start(bf16[64,3072]{1,0:T(8,128)(2,1)S(1)} %pad_maximum_fusion.2), channel_id=1, source_target_pairs={{0,1},{1,2},{2,3},{3,0},{8,9},{9,10},{10,11},{11,8},{16,17},{17,18... | collective-permute-start | bytes 1179656 | tf_op jit(solution)/shard_map/ppermute | solution.py:20
  121.4 8.6 %collective-permute-start.24 = (bf16[64,3072]{1,0:T(8,128)(2,1)S(1)}, bf16[64,3072]{1,0:T(8,128)(2,1)S(1)}, u32[]{:S(2)}, u32[]{:S(2)}) collective-permute-start(bf16[64,3072]{1,0:T(8,128)(2,1)S(1)} %pad_maximum_fusion.3), channel_id=1, source_target_pairs={{0,3},{1,0},{2,1},{3,2},{8,11},{9,8},{10,9},{11,10},{16,19},{17,16... | collective-permute-start | bytes 1179656 | tf_op jit(solution)/shard_map/ppermute | solution.py:20
  130.0 9.1 %collective-permute-start.25 = (bf16[64,3072]{1,0:T(8,128)(2,1)S(1)}, bf16[64,3072]{1,0:T(8,128)(2,1)S(1)}, u32[]{:S(2)}, u32[]{:S(2)}) collective-permute-start(bf16[64,3072]{1,0:T(8,128)(2,1)S(1)} %fusion.55), channel_id=1, source_target_pairs={{0,3},{1,0},{2,1},{3,2},{8,11},{9,8},{10,9},{11,10},{16,19},{17,16... | collective-permute-start | bytes 1179656 | tf_op jit(solution)/shard_map/ppermute | solution.py:20
  (14 other events, 190.1 us)
